TPU v7x, 32 devices: a whole 2x2x4 slice. The times are simulated.
32 devices in a mesh: row: 4 (over z), col: 4 (over y, x), rep: 2 (over core).
Axes of the slice: x: 2, y: 2, z: 4, core: 2. Of those that a mesh axis runs over, the one named last changes fastest.
Arguments:
- pair: bfloat16 [512, 512, 128], P('row', 'col'), may hold values from -8 to 8
- w_left: bfloat16 [2, 128, 128], P(None, None, 'rep'), may hold values from -1 to 1
- w_left_gate: bfloat16 [2, 128, 128], P(None, None, 'rep'), may hold values from -0.5 to 0.5
- w_right: bfloat16 [2, 128, 128], P(None, None, 'rep'), may hold values from -0.5 to 0.5
- w_right_gate: bfloat16 [2, 128, 128], P(None, None, 'rep'), may hold values from -0.5 to 0.5
- w_gate: bfloat16 [2, 128, 128], replicated, may hold values from -0.5 to 0.5
- w_out: bfloat16 [2, 128, 128], P(None, 'rep'), may hold values from -0.5 to 0.5
- w_trans_in: bfloat16 [128, 1024], replicated, may hold values from -0.5 to 0.5
- w_trans_out: bfloat16 [512, 128], replicated, may hold values from -0.25 to 0.25
Outputs:
- updated: bfloat16 [512, 512, 128], P('row', ('col', 'rep'))
All inputs are finite; a program needn't handle non-finite values.
Results may differ from a plain program's by a relative error of at most 0.013.
Values may be sent and summed in bfloat16 or wider, within the bound.
A program may use at most 192 MiB of HBM per device.

v0:
```python
import functools

import jax
import jax.numpy as jnp
from jax import lax
from jax.experimental import pallas as pl
from jax.experimental.pallas import tpu as pltpu
from jax.sharding import PartitionSpec as P

epsilon = 1e-05
ALL = ("row", "col", "rep")
MESH = pl.DeviceIdType.MESH
GROUPS = 8
AHEAD = 2
LAG = 2


def triangle_kernel(
    outgoing, cols, reps, groups,
    lr_ref, out_ref,
    own, far, outb, inb, hid, got,
    local_sem, in_send, in_recv, ret_local, ret_send, ret_recv, z_send, z_recv,
):
    members = cols * reps
    channels = lr_ref.shape[1]
    per = channels // groups
    width = lr_ref.shape[3]
    height = lr_ref.shape[4]
    row, col, rep = (lax.axis_index(name) for name in ALL)
    me = col * reps + rep
    half = row // 2
    is_mid = (row == 1) | (row == 2)
    mate = half * 4 + 1 - row
    across = 3 - row
    own_index = 0 if outgoing else 1 - half
    far_index = 1 if outgoing else half

    def member(offset):
        return lax.rem(me + offset, members)

    def place(index):
        return (row, index // reps, lax.rem(index, reps))

    barrier = pltpu.get_barrier_semaphore()
    for offset in range(1, members):
        pl.semaphore_signal(barrier, inc=1, device_id=place(member(offset)), device_id_type=MESH)
    pl.semaphore_signal(barrier, inc=1, device_id=(mate, col, rep), device_id_type=MESH)

    @pl.when(is_mid)
    def _():
        pl.semaphore_signal(barrier, inc=1, device_id=(across, col, rep), device_id_type=MESH)

    pl.semaphore_wait(barrier, jnp.where(is_mid, members + 1, members))

    def group(g):
        return pl.ds(g * per, per)

    def strip(index):
        return pl.ds(pl.multiple_of(index * width, width), width)

    def spread(g, offset):
        dest = member(offset)
        return pltpu.make_async_remote_copy(
            src_ref=lr_ref.at[dest, group(g)],
            dst_ref=own.at[group(g), :, strip(me)],
            send_sem=in_send.at[g, offset],
            recv_sem=in_recv.at[g, offset],
            device_id=place(dest),
            device_id_type=MESH,
        )

    def spread_local(g):
        return pltpu.make_async_copy(
            lr_ref.at[me, group(g)], own.at[group(g), :, strip(me)], local_sem.at[g]
        )

    def give_back(g, offset, source):
        dest = member(offset)
        return pltpu.make_async_remote_copy(
            src_ref=source.at[group(g), strip(dest)],
            dst_ref=out_ref.at[pl.ds(me * channels + g * per, per)],
            send_sem=ret_send.at[g, offset],
            recv_sem=ret_recv.at[g, offset],
            device_id=place(dest),
            device_id_type=MESH,
        )

    def give_back_local(g, source):
        return pltpu.make_async_copy(
            source.at[group(g), strip(me)],
            out_ref.at[pl.ds(me * channels + g * per, per)],
            ret_local.at[g],
        )

    def along(g, kind, source, target, to):
        return pltpu.make_async_remote_copy(
            src_ref=source,
            dst_ref=target,
            send_sem=z_send.at[kind, g],
            recv_sem=z_recv.at[kind, g],
            device_id=(to, col, rep),
            device_id_type=MESH,
        )

    def to_middle(g):
        return along(g, 0, own.at[group(g)], far.at[group(g)], mate)

    def across_first(g):
        if outgoing:
            return along(g, 1, own.at[group(g), 1], inb.at[0, group(g)], across)
        return along(g, 1, outb.at[group(g)], inb.at[group(g)], across)

    def across_second(g):
        return along(g, 2, far.at[group(g), 1], inb.at[1, group(g)], across)

    def to_end(g):
        return along(g, 3, hid.at[far_index, group(g)], got.at[group(g)], mate)

    def start_spread(g):
        spread_local(g).start()
        for offset in range(1, members):
            spread(g, offset).start()

    def wait_spread(g):
        spread_local(g).wait()
        for offset in range(1, members):
            spread(g, offset).wait_recv()

    def start_back(g, source):
        give_back_local(g, source).start()
        for offset in range(1, members):
            give_back(g, offset, source).start()

    def finish_back(g, source):
        give_back_local(g, source).wait()
        for offset in range(1, members):
            give_back(g, offset, source).wait()
            spread(g, offset).wait_send()

    for g in range(min(AHEAD, groups)):
        start_spread(g)

    def joined(c, side, rows):
        return jnp.concatenate([own[c, side, rows], far[c, side, rows]], axis=1)

    everything = pl.ds(0, members * width)

    def partial(c, which):
        rows = pl.ds(pl.multiple_of(which * 2 * height, 2 * height), 2 * height)
        return lax.dot_general(
            joined(c, 1, everything),
            joined(c, 0, rows),
            (((1,), (1,)), ((), ())),
            preferred_element_type=jnp.float32,
        )

    def forward(c):
        outb[c] = partial(c, 1 - half).astype(outb.dtype)

    def multiply(c):
        if outgoing:
            left = joined(c, 0, everything)
            blocks = (
                (row, own.at[c, 1]),
                (mate, far.at[c, 1]),
                (across, inb.at[0, c]),
                (3 - mate, inb.at[1, c]),
            )
            for block, right in blocks:
                result = lax.dot_general(
                    right[...],
                    left,
                    (((0,), (0,)), ((), ())),
                    preferred_element_type=jnp.float32,
                ).astype(hid.dtype)
                rows = pl.ds(pl.multiple_of(block * height, height), height)
                hid[0, c, rows] = result[:, :height]
                hid[1, c, rows] = result[:, height:]
        else:
            result = (partial(c, half) + inb[c].astype(jnp.float32)).astype(hid.dtype)
            hid[0, c] = result[:, :height]
            hid[1, c] = result[:, height:]

    def each(g, func):
        lax.fori_loop(0, per, lambda n, _: (func(g * per + n), _)[1], 0)

    @pl.when(is_mid)
    def _():
        back = hid.at[own_index]

        def step(m, carry):
            @pl.when(m + AHEAD < groups)
            def _():
                start_spread(m + AHEAD)

            @pl.when(m < groups)
            def _():
                wait_spread(m)
                if outgoing:
                    across_first(m).start()

            @pl.when((m >= 1) & (m <= groups))
            def _():
                g = m - 1
                to_middle(g).wait_recv()
                if outgoing:
                    across_second(g).start()
                else:
                    each(g, forward)
                    across_first(g).start()

            @pl.when(m >= 2)
            def _():
                g = m - 2
                across_first(g).wait_recv()
                if outgoing:
                    across_second(g).wait_recv()
                each(g, multiply)
                to_end(g).start()
                start_back(g, back)

            return carry

        lax.fori_loop(0, groups + 2, step, 0)

        def drain(g, carry):
            finish_back(g, back)
            across_first(g).wait_send()
            if outgoing:
                across_second(g).wait_send()
            to_end(g).wait_send()
            return carry

        lax.fori_loop(0, groups, drain, 0)

    @pl.when(jnp.logical_not(is_mid))
    def _():
        def step(m, carry):
            @pl.when(m + AHEAD < groups)
            def _():
                start_spread(m + AHEAD)

            @pl.when(m < groups)
            def _():
                wait_spread(m)
                to_middle(m).start()

            @pl.when(m >= LAG)
            def _():
                to_end(m - LAG).wait_recv()
                start_back(m - LAG, got)

            return carry

        lax.fori_loop(0, groups + LAG, step, 0)

        def drain(g, carry):
            finish_back(g, got)
            to_middle(g).wait_send()
            return carry

        lax.fori_loop(0, groups, drain, 0)


def triangle_line(lr, outgoing):
    cols, reps = lax.axis_size("col"), lax.axis_size("rep")
    members, channels, _, width, height = lr.shape
    groups = min(GROUPS, channels)
    long, npair = members * width, 4 * height
    bf16 = jnp.bfloat16
    dma = pltpu.SemaphoreType.DMA
    return pl.pallas_call(
        functools.partial(triangle_kernel, outgoing, cols, reps, groups),
        out_shape=jax.ShapeDtypeStruct((members * channels, width, height), bf16),
        in_specs=[pl.BlockSpec(memory_space=pltpu.VMEM)],
        out_specs=pl.BlockSpec(memory_space=pltpu.VMEM),
        scratch_shapes=[
            pltpu.VMEM((channels, 2, long, height), bf16),
            pltpu.VMEM((channels, 2, long, height), bf16),
            pltpu.VMEM((16, 128) if outgoing else (channels, long, 2 * height), bf16),
            pltpu.VMEM(
                (2, channels, long, height) if outgoing else (channels, long, 2 * height), bf16
            ),
            pltpu.VMEM((2, channels, npair, height), bf16),
            pltpu.VMEM((channels, npair, height), bf16),
            dma((groups,)),
            dma((groups, members)),
            dma((groups, members)),
            dma((groups,)),
            dma((groups, members)),
            dma((groups, members)),
            dma((4, groups)),
            dma((4, groups)),
        ],
        compiler_params=pltpu.CompilerParams(
            collective_id=1 if outgoing else 2,
            has_side_effects=True,
            vmem_limit_bytes=48 * 2**20,
        ),
        cost_estimate=pl.CostEstimate(
            flops=4 * channels * npair * npair * height,
            bytes_accessed=6 * lr.size,
            transcendentals=0,
        ),
        name="triangle_out" if outgoing else "triangle_in",
    )(lr)


def exchange(values, axes):
    return lax.all_to_all(values, axes, split_axis=0, concat_axis=0, tiled=True)


def triangle_any(lr, outgoing):
    rows = lax.axis_size("row")
    members, channels, _, width, height = lr.shape
    per = channels // rows
    grid = lr.reshape(members, rows, per, 2, width, height)
    got = exchange(jnp.moveaxis(grid, 1, 0).reshape(rows * members, per, 2, width, height), ALL)
    grid = got.reshape(rows, members, per, 2, width, height)
    full = jnp.transpose(grid, (3, 2, 1, 4, 0, 5)).reshape(
        2, per, members * width, rows * height
    )
    form = "cka,ckb->cba" if outgoing else "cak,cbk->cba"
    products = jnp.einsum(form, full[0], full[1], preferred_element_type=jnp.float32)
    grid = products.astype(jnp.bfloat16).reshape(per, members, width, rows, height)
    outbound = jnp.transpose(grid, (3, 1, 0, 2, 4)).reshape(-1, per, width, height)
    back = exchange(outbound, ALL).reshape(rows, members, per, width, height)
    return jnp.moveaxis(back, 0, 1).reshape(members * channels, width, height)


def triangle(lr, outgoing):
    if lax.axis_size("row") == 4 and lr.shape[1] % min(GROUPS, lr.shape[1]) == 0:
        return triangle_line(lr, outgoing)
    return triangle_any(lr, outgoing)


def normalize(values, axis):
    mean_value = jnp.mean(values, axis, keepdims=True)
    square_mean = jnp.mean(values * values, axis, keepdims=True)
    return (values - mean_value) * lax.rsqrt(square_mean - mean_value * mean_value + epsilon)


def gated(normed, w_value, w_gate):
    value = jnp.einsum("abd,dc->cab", normed, w_value, preferred_element_type=jnp.float32)
    gate = jnp.einsum("abd,dc->cab", normed, w_gate, preferred_element_type=jnp.float32)
    return (jax.nn.sigmoid(gate) * value).astype(jnp.bfloat16)


def finish(state, normed, returned, w_gate, w_out):
    scaled = normalize(returned.astype(jnp.float32), 0).astype(jnp.bfloat16)
    projected = jnp.einsum("cji,cd->jid", scaled, w_out, preferred_element_type=jnp.float32)
    gate = jax.nn.sigmoid(
        jnp.einsum("jid,de->jie", normed, w_gate, preferred_element_type=jnp.float32)
    )
    return state + gate * projected


def spread_tile(normed, w_left, w_left_gate, w_right, w_right_gate):
    members = lax.axis_size("col") * lax.axis_size("rep")
    pairs = jnp.stack(
        [gated(normed, w_left, w_left_gate), gated(normed, w_right, w_right_gate)], axis=1
    )
    return pairs.reshape(members, -1, *pairs.shape[1:])


def on_device(
    pair, w_left, w_left_gate, w_right, w_right_gate, w_gate, w_out, w_trans_in, w_trans_out
):
    reps = lax.axis_size("rep")
    width = pair.shape[1] // reps
    out_all = lax.all_gather(w_out, "rep", axis=1, tiled=True)
    sides = lax.all_gather(
        jnp.stack([w_left, w_left_gate, w_right, w_right_gate]), "rep", axis=3, tiled=True
    )
    half = lax.dynamic_slice_in_dim(pair, lax.axis_index("rep") * width, width, 1)
    state = jnp.transpose(half, (1, 0, 2)).astype(jnp.float32)
    for index, outgoing in ((0, True), (1, False)):
        normed = normalize(state, 2).astype(jnp.bfloat16)
        lr = spread_tile(normed, *(sides[n, index] for n in range(4)))
        returned = triangle(lr, outgoing)
        state = finish(state, normed, returned, w_gate[index], out_all[index])

    normed = normalize(state, 2).astype(jnp.bfloat16)
    hidden = w_trans_out.shape[0]
    inner = jnp.einsum("jid,de->jie", normed, w_trans_in, preferred_element_type=jnp.float32)
    active = (jax.nn.silu(inner[..., :hidden]) * inner[..., hidden:]).astype(jnp.bfloat16)
    updated = state + jnp.einsum(
        "jie,ed->jid", active, w_trans_out, preferred_element_type=jnp.float32
    )
    return jnp.transpose(updated.astype(jnp.bfloat16), (1, 0, 2))


def solution(mesh):
    placed = (
        P("row", "col", None),
        P(None, None, "rep"),
        P(None, None, "rep"),
        P(None, None, "rep"),
        P(None, None, "rep"),
        P(),
        P(None, "rep", None),
        P(),
        P(),
    )
    return jax.shard_map(
        on_device,
        mesh=mesh,
        in_specs=placed,
        out_specs=P("row", ("col", "rep"), None),
        check_vma=False,
    )
```

profile of v0, /device:TPU:0, one launch (start us, length us, event | category | flops | bytes accessed | tf_op | source)
XLA Modules:
  0.0 356.2 jit_solution(17604184017118389186)
XLA Ops:
  0.8 2.0 all_gather.7
  3.1 0.8 pad_maximum_fusion.2
  4.0 2.0 all_gather.6
  6.0 3.1 constant_dynamic-slice_fusion
  9.1 3.3 copy.70
  12.4 1.2 fusion.6
  14.4 1.7 multiply_convert_fusion.5
  16.1 1.4 copy.38
  18.2 1.7 multiply_convert_fusion.4
  19.9 1.4 copy.41
  21.2 2.3 pad_maximum_fusion.lr_ref
  23.5 139.2 %triangle_out.1 = bf16[128,64,128]{2,1,0:T(8,128)(2,1)S(1)} custom-call(bf16[8,16,2,64,128]{4,3,2,1,0:T(8,128)(2,1)} %pad_maximum_fusion.lr_ref), custom_call_target="tpu_custom_call" | custom-call | flops 2147483648 | bytes 12582912 | tf_op jit(solution)/shard_map/triangle_out/pallas_call | solution.py:272
  164.9 5.8 %fusion.27 = (f32[64,128]{1,0:T(8,128)S(1)}, f32[64,128]{1,0:T(8,128)S(1)}, f32[64,128,128]{1,2,0:T(8,128)S(1)}) fusion(bf16[128,64,128]{0,2,1:T(8,128)(2,1)S(1)} %copy.70, bf16[128,64,128]{2,1,0:T(8,128)(2,1)S(1)} %fusion.14, bf16[1,128,128]{1,2,0:T(8,128)(2,1)S(1)} %copy.72, f32[64,128,128]{1,2,0:T(8,128)S(1)} %fusion.36), kind=kOutput, calls=%fused_computation.45 | convolution fusion | flops 277856256 | bytes 12681216 | tf_op jit(solution)/shard_map/cji,cd->jid/dot_general | solution.py:351
  170.7 1.0 multiply_convert_fusion.3
  172.3 1.4 multiply_convert_fusion.1
  173.7 1.4 copy.52
  175.8 1.4 multiply_convert_fusion.2
  177.2 1.4 copy.49
  178.6 2.3 pad_maximum_fusion.1.lr_ref
  180.9 131.2 %triangle_in.1 = bf16[128,64,128]{2,1,0:T(8,128)(2,1)S(1)} custom-call(bf16[8,16,2,64,128]{4,3,2,1,0:T(8,128)(2,1)} %pad_maximum_fusion.1.lr_ref), custom_call_target="tpu_custom_call" | custom-call | flops 2147483648 | bytes 12582912 | tf_op jit(solution)/shard_map/triangle_in/pallas_call | solution.py:272
  314.2 7.2 %fusion.48 = (f32[64,128]{1,0:T(8,128)S(1)}, f32[64,128]{1,0:T(8,128)S(1)}, f32[64,128,128]{1,2,0:T(8,128)S(1)}, f32[64,128,128]{1,2,0:T(8,128)}) fusion(f32[64,128,128]{1,2,0:T(8,128)S(1)} %get-tuple-element.28, bf16[128,64,128]{0,2,1:T(8,128)(2,1)S(1)} %copy.70, bf16[128,64,128]{2,1,0:T(8,128)(2,1)S(1)} %fusion.17, bf16[1,128,128]{1,2,0:T(8,128)(2,1)S(1)} %copy.74, ...), kind=kOutput, calls=%fused_computation.81 | convolution fusion | flops 278904832 | bytes 21069824 | tf_op jit(solution)/shard_map/cji,cd->jid/dot_general | solution.py:351
  321.4 13.1 %fusion.21 = f32[64,128,1024]{2,1,0:T(8,128)} fusion(f32[64,128,128]{1,2,0:T(8,128)S(1)} %get-tuple-element.15, f32[64,128]{1,0:T(8,128)S(1)} %get-tuple-element.19, f32[64,128]{1,0:T(8,128)S(1)} %get-tuple-element.18, bf16[128,1024]{1,0:T(8,128)(2,1)S(1)} %copy-done), kind=kOutput, calls=%fused_computation.39 | convolution fusion | flops 2150629376 | bytes 38076416 | tf_op jit(solution)/shard_map/jid,de->jie/dot_general | solution.py:385
  334.5 17.2 %fusion.12 = bf16[128,64,128]{0,2,1:T(8,128)(2,1)} fusion(bf16[128,64,128]{0,2,1:T(8,128)(2,1)S(1)} %copy.70, f32[64,128,128]{1,2,0:T(8,128)} %get-tuple-element.29, f32[64,128,128]{1,2,0:T(8,128)} %copy-done.1, f32[64,128,1024]{2,1,0:T(8,128)} %fusion.21, bf16[512,128]{1,0:T(8,128)(2,1)S(1)} %copy-done.3), kind=kOutput, calls=%fused_computation.20 | convolution fusion | flops 1104150528 | bytes 46268416 | tf_op jit(solution)/shard_map/jie,ed->jid/dot_general | solution.py:387
  351.7 4.1 %copy.57 = bf16[128,64,128]{2,1,0:T(8,128)(2,1)} copy(bf16[128,64,128]{0,2,1:T(8,128)(2,1)} %fusion.12) | data formatting | bytes 4194304 | tf_op jit(solution)/shard_map/convert_element_type | solution.py:390
  (27 shorter events, 8.2 us)
Async XLA Ops:
  0.0 321.4 %copy-start = (bf16[128,1024]{1,0:T(8,128)(2,1)S(1)}, bf16[128,1024]{1,0:T(8,128)(2,1)}, u32[]{:S(2)}) copy-start(bf16[128,1024]{1,0:T(8,128)(2,1)} %param.16) | copy-start | bytes 786436
  162.7 1.4 copy-start.2
  170.6 143.5 %copy-start.1 = (f32[64,128,128]{1,2,0:T(8,128)}, f32[64,128,128]{1,2,0:T(8,128)S(1)}, u32[]{:S(2)}) copy-start(f32[64,128,128]{1,2,0:T(8,128)S(1)} %get-tuple-element.28) | copy-start | bytes 12582916
  321.4 13.1 %copy-start.3 = (bf16[512,128]{1,0:T(8,128)(2,1)S(1)}, bf16[512,128]{1,0:T(8,128)(2,1)}, u32[]{:S(2)}) copy-start(bf16[512,128]{1,0:T(8,128)(2,1)} %param.17) | copy-start | bytes 393220
where the time goes:
time: 359 us; the launch traced here: 356 us
  Pallas kernels  270 us (75%)
  matrix products  53.7 us (15%)
  local copies, waits for them, and re-layouts  17.1 us (5%)
  other arithmetic  10.4 us (3%)
  blocking collectives  3.95 us (1%)
    pallas_call x2, Pallas kernels, triangle_line(): pl.pallas_call(functools.partial(triangle_kernel, outgoing, cols, reps, g...  270 us
    dot_general x1, matrix products, on_device(): jnp.einsum('jie,ed->jid', active, w_trans_out, preferred_element_type=jnp...  17.2 us
    dot_general x1, matrix products, on_device(): jnp.einsum('jid,de->jie', normed, w_trans_in, preferred_element_type=jnp....  13.1 us
    dot_general x2, matrix products, finish(): jnp.einsum('cji,cd->jid', scaled, w_out, preferred_element_type=jnp.float32)  12.9 us

commit v1 on v0

--- a/solution.py
+++ b/solution.py
@@ -11,8 +11,7 @@
 ALL = ("row", "col", "rep")
 MESH = pl.DeviceIdType.MESH
 GROUPS = 8
-AHEAD = 2
-LAG = 2
+LAG = 3
 
 
 def triangle_kernel(
@@ -103,7 +102,12 @@
         )
 
     def to_middle(g):
+        if outgoing:
+            return along(g, 0, own.at[group(g), 1], far.at[group(g), 1], mate)
         return along(g, 0, own.at[group(g)], far.at[group(g)], mate)
+
+    def to_middle_left(g):
+        return along(g, 4, own.at[group(g), 0], far.at[group(g), 0], mate)
 
     def across_first(g):
         if outgoing:
@@ -137,8 +141,7 @@
             give_back(g, offset, source).wait()
             spread(g, offset).wait_send()
 
-    for g in range(min(AHEAD, groups)):
-        start_spread(g)
+    start_spread(0)
 
     def joined(c, side, rows):
         return jnp.concatenate([own[c, side, rows], far[c, side, rows]], axis=1)
@@ -189,15 +192,15 @@
         back = hid.at[own_index]
 
         def step(m, carry):
-            @pl.when(m + AHEAD < groups)
-            def _():
-                start_spread(m + AHEAD)
-
             @pl.when(m < groups)
             def _():
                 wait_spread(m)
                 if outgoing:
                     across_first(m).start()
+
+            @pl.when(m + 1 < groups)
+            def _():
+                start_spread(m + 1)
 
             @pl.when((m >= 1) & (m <= groups))
             def _():
@@ -214,6 +217,7 @@
                 g = m - 2
                 across_first(g).wait_recv()
                 if outgoing:
+                    to_middle_left(g).wait_recv()
                     across_second(g).wait_recv()
                 each(g, multiply)
                 to_end(g).start()
@@ -236,14 +240,16 @@
     @pl.when(jnp.logical_not(is_mid))
     def _():
         def step(m, carry):
-            @pl.when(m + AHEAD < groups)
-            def _():
-                start_spread(m + AHEAD)
-
             @pl.when(m < groups)
             def _():
                 wait_spread(m)
                 to_middle(m).start()
+                if outgoing:
+                    to_middle_left(m).start()
+
+            @pl.when(m + 1 < groups)
+            def _():
+                start_spread(m + 1)
 
             @pl.when(m >= LAG)
             def _():
@@ -257,6 +263,8 @@
         def drain(g, carry):
             finish_back(g, got)
             to_middle(g).wait_send()
+            if outgoing:
+                to_middle_left(g).wait_send()
             return carry
 
         lax.fori_loop(0, groups, drain, 0)
@@ -289,8 +297,8 @@
             dma((groups,)),
             dma((groups, members)),
             dma((groups, members)),
-            dma((4, groups)),
-            dma((4, groups)),
+            dma((5, groups)),
+            dma((5, groups)),
         ],
         compiler_params=pltpu.CompilerParams(
             collective_id=1 if outgoing else 2,
@@ -340,12 +348,6 @@
     return (values - mean_value) * lax.rsqrt(square_mean - mean_value * mean_value + epsilon)
 
 
-def gated(normed, w_value, w_gate):
-    value = jnp.einsum("abd,dc->cab", normed, w_value, preferred_element_type=jnp.float32)
-    gate = jnp.einsum("abd,dc->cab", normed, w_gate, preferred_element_type=jnp.float32)
-    return (jax.nn.sigmoid(gate) * value).astype(jnp.bfloat16)
-
-
 def finish(state, normed, returned, w_gate, w_out):
     scaled = normalize(returned.astype(jnp.float32), 0).astype(jnp.bfloat16)
     projected = jnp.einsum("cji,cd->jid", scaled, w_out, preferred_element_type=jnp.float32)
@@ -355,12 +357,97 @@
     return state + gate * projected
 
 
-def spread_tile(normed, w_left, w_left_gate, w_right, w_right_gate):
-    members = lax.axis_size("col") * lax.axis_size("rep")
-    pairs = jnp.stack(
-        [gated(normed, w_left, w_left_gate), gated(normed, w_right, w_right_gate)], axis=1
-    )
-    return pairs.reshape(members, -1, *pairs.shape[1:])
+def squash(values):
+    return 0.5 * jnp.tanh(0.5 * values) + 0.5
+
+
+def project_kernel(state_ref, weight_ref, normed_ref, lr_ref, turned):
+    channels = lr_ref.shape[0]
+    normed = normalize(state_ref[...], 2).astype(jnp.bfloat16)
+    normed_ref[...] = normed
+    for n in range(normed.shape[0]):
+        linear = lax.dot_general(
+            weight_ref[...],
+            normed[n],
+            (((1,), (1,)), ((), ())),
+            preferred_element_type=jnp.float32,
+        )
+        for side in range(2):
+            first = 2 * side * channels
+            value = linear[first : first + channels]
+            gate = linear[first + channels : first + 2 * channels]
+            turned[:, side, n, :] = squash(gate) * value
+    lr_ref[...] = turned[...].astype(lr_ref.dtype)
+
+
+def project(state, weight):
+    width, height, depth = state.shape
+    channels = weight.shape[0] // 4
+    block = 8
+    return pl.pallas_call(
+        project_kernel,
+        grid=(width // block,),
+        out_shape=(
+            jax.ShapeDtypeStruct(state.shape, jnp.bfloat16),
+            jax.ShapeDtypeStruct((channels, 2, width, height), jnp.bfloat16),
+        ),
+        in_specs=[
+            pl.BlockSpec((block, height, depth), lambda n: (n, 0, 0)),
+            pl.BlockSpec(weight.shape, lambda n: (0, 0)),
+        ],
+        out_specs=(
+            pl.BlockSpec((block, height, depth), lambda n: (n, 0, 0)),
+            pl.BlockSpec((channels, 2, block, height), lambda n: (0, 0, n, 0)),
+        ),
+        scratch_shapes=[pltpu.VMEM((channels, 2, block, height), jnp.float32)],
+        compiler_params=pltpu.CompilerParams(vmem_limit_bytes=40 * 2**20),
+        cost_estimate=pl.CostEstimate(
+            flops=2 * state.size * weight.shape[0],
+            bytes_accessed=10 * state.size,
+            transcendentals=2 * state.size,
+        ),
+        name="project",
+    )(state, weight)
+
+
+def transition_kernel(state_ref, w_in_ref, w_out_ref, out_ref, turned):
+    block, height, depth = state_ref.shape
+    hidden = w_out_ref.shape[0]
+    state = state_ref[...].reshape(block * height, depth)
+    normed = normalize(state, 1).astype(jnp.bfloat16)
+    inner = jnp.dot(normed, w_in_ref[...], preferred_element_type=jnp.float32)
+    gate = inner[:, :hidden]
+    active = gate * squash(gate) * inner[:, hidden:]
+    updated = state + jnp.dot(
+        active.astype(jnp.bfloat16), w_out_ref[...], preferred_element_type=jnp.float32
+    )
+    for n in range(block):
+        turned[:, n, :] = updated[n * height : (n + 1) * height]
+    out_ref[...] = turned[...].astype(out_ref.dtype)
+
+
+def transition(state, w_trans_in, w_trans_out):
+    width, height, depth = state.shape
+    block = 8
+    return pl.pallas_call(
+        transition_kernel,
+        grid=(width // block,),
+        out_shape=jax.ShapeDtypeStruct((height, width, depth), jnp.bfloat16),
+        in_specs=[
+            pl.BlockSpec((block, height, depth), lambda n: (n, 0, 0)),
+            pl.BlockSpec(w_trans_in.shape, lambda n: (0, 0)),
+            pl.BlockSpec(w_trans_out.shape, lambda n: (0, 0)),
+        ],
+        out_specs=pl.BlockSpec((height, block, depth), lambda n: (0, n, 0)),
+        scratch_shapes=[pltpu.VMEM((height, block, depth), jnp.float32)],
+        compiler_params=pltpu.CompilerParams(vmem_limit_bytes=40 * 2**20),
+        cost_estimate=pl.CostEstimate(
+            flops=6 * state.size * w_trans_out.shape[0],
+            bytes_accessed=6 * state.size,
+            transcendentals=state.size * w_trans_out.shape[0] // depth,
+        ),
+        name="transition",
+    )(state, w_trans_in, w_trans_out)
 
 
 def on_device(
@@ -374,20 +461,13 @@
     )
     half = lax.dynamic_slice_in_dim(pair, lax.axis_index("rep") * width, width, 1)
     state = jnp.transpose(half, (1, 0, 2)).astype(jnp.float32)
+    members = lax.axis_size("col") * reps
+    weights = jnp.transpose(sides, (1, 0, 3, 2)).reshape(2, -1, sides.shape[2])
     for index, outgoing in ((0, True), (1, False)):
-        normed = normalize(state, 2).astype(jnp.bfloat16)
-        lr = spread_tile(normed, *(sides[n, index] for n in range(4)))
-        returned = triangle(lr, outgoing)
+        normed, lr = project(state, weights[index])
+        returned = triangle(lr.reshape(members, -1, *lr.shape[1:]), outgoing)
         state = finish(state, normed, returned, w_gate[index], out_all[index])
-
-    normed = normalize(state, 2).astype(jnp.bfloat16)
-    hidden = w_trans_out.shape[0]
-    inner = jnp.einsum("jid,de->jie", normed, w_trans_in, preferred_element_type=jnp.float32)
-    active = (jax.nn.silu(inner[..., :hidden]) * inner[..., hidden:]).astype(jnp.bfloat16)
-    updated = state + jnp.einsum(
-        "jie,ed->jid", active, w_trans_out, preferred_element_type=jnp.float32
-    )
-    return jnp.transpose(updated.astype(jnp.bfloat16), (1, 0, 2))
+    return transition(state, w_trans_in, w_trans_out)
 
 
 def solution(mesh):

time: 359 us -> 311 us (0.87)
  matrix products: 53.7 us -> 9.43 us
  Pallas kernels: 270 us -> 288 us
  local copies, waits for them, and re-layouts: 17.1 us -> 5.74 us
  other arithmetic: 10.4 us -> 3.84 us
    dot_general x10 -> x0, matrix products: 39.3 us -> none  [the longest x1 17.2 us: on_device(): jnp.einsum('jie,ed->jid', active, w_trans_out, preferred_element_type=jnp...]
    pallas_call x0 -> x3, Pallas kernels: none -> 33.5 us  [the longest x2 22.3 us: project(): pl.pallas_call(project_kernel, grid=(width // block,), out_shape=(jax.Sha...]
    pallas_call x2, Pallas kernels: 270 us -> 254 us  [triangle_line(): pl.pallas_call(functools.partial(triangle_kernel, outgoing, cols, reps, g...]
    convert_element_type x5 -> x0, local copies, waits for them, and re-layouts: 9.52 us -> none  [the longest x4 5.42 us: gated(): return (jax.nn.sigmoid(gate) * value).astype(jnp.bfloat16)]
    dot_general x2, matrix products: 12.9 us -> 8.06 us  [finish(): jnp.einsum('cji,cd->jid', scaled, w_out, preferred_element_type=jnp.float32)]
    another operation x2 -> x0, other arithmetic: 4.6 us -> none  [spread_tile(): jnp.stack([gated(normed, w_left, w_left_gate), gated(normed, w_right, w_r...]
where the time goes in v1:
time: 311 us
  Pallas kernels  288 us (93%)
  matrix products  9.43 us (3%)
  local copies, waits for them, and re-layouts  5.74 us (2%)
  blocking collectives  4.11 us (1%)
  other arithmetic  3.84 us (1%)
    pallas_call x2, Pallas kernels, triangle_line(): pl.pallas_call(functools.partial(triangle_kernel, outgoing, cols, reps, g...  254 us
    pallas_call x2, Pallas kernels, project(): pl.pallas_call(project_kernel, grid=(width // block,), out_shape=(jax.Sha...  22.3 us
    pallas_call x1, Pallas kernels, transition(): pl.pallas_call(transition_kernel, grid=(width // block,), out_shape=jax.S...  11.2 us
    dot_general x2, matrix products, finish(): jnp.einsum('cji,cd->jid', scaled, w_out, preferred_element_type=jnp.float32)  8.06 us

profile of v1, /device:TPU:0, one launch (start us, length us, event | category | flops | bytes accessed | tf_op | source)
XLA Modules:
  0.0 311.2 jit_solution(17410782512126939517)
XLA Ops:
  0.0 1.8 constant_dynamic-slice_fusion
  1.8 0.0 copy-start.6
  1.8 0.0 copy-start.8
  1.8 0.0 copy-start.9
  1.8 1.2 convert_bitcast_fusion.state_ref
  3.1 2.1 all_gather.6
  5.2 11.1 %project.2 = (bf16[64,128,128]{2,1,0:T(8,128)(2,1)S(1)}, bf16[128,2,64,128]{3,2,1,0:T(8,128)(2,1)S(1)}) custom-call(f32[64,128,128]{2,1,0:T(8,128)S(1)} %convert_bitcast_fusion.state_ref, bf16[512,128]{1,0:T(8,128)(2,1)S(1)} %bitcast.32), custom_call_target="tpu_custom_call" | custom-call | flops 1073741824 | bytes 10485760 | tf_op jit(solution)/shard_map/project/pallas_call | solution.py:387
  16.4 1.9 copy-done
  18.3 123.7 %triangle_out.1 = bf16[128,64,128]{2,1,0:T(8,128)(2,1)S(1)} custom-call(bf16[8,16,2,64,128]{4,3,2,1,0:T(8,128)(2,1)} %bitcast.33), custom_call_target="tpu_custom_call" | custom-call | flops 2147483648 | bytes 12582912 | tf_op jit(solution)/shard_map/triangle_out/pallas_call | solution.py:280
  142.1 0.0 copy-start.4
  142.1 0.6 convert_reduce_fusion.1
  142.7 0.7 fusion.1
  143.4 0.7 fusion.10
  144.1 0.0 copy-done.5
  144.1 2.0 all_gather.7
  146.2 5.1 %multiply_add_fusion.1.state_ref = f32[64,128,128]{2,1,0:T(8,128)S(1)} fusion(f32[64,128,128]{2,1,0:T(8,128)S(1)} %fusion.10, bf16[128,64,128]{2,1,0:T(8,128)(2,1)S(1)} %fusion.1, bf16[128,64,128]{2,1,0:T(8,128)(2,1)S(1)} %constant_dynamic-slice_fusion, bf16[2,128,128]{2,1,0:T(8,128)(2,1)S(1)} %all_gather.7), kind=kOutput, calls=%fused_computation.14 | convolution fusion | flops 274726912 | bytes 12615680 | tf_op jit(solution)/shard_map/cji,cd->jid/dot_general | solution.py:353
  151.2 11.1 %project.3 = (bf16[64,128,128]{2,1,0:T(8,128)(2,1)S(1)}, bf16[128,2,64,128]{3,2,1,0:T(8,128)(2,1)S(1)}) custom-call(f32[64,128,128]{2,1,0:T(8,128)S(1)} %multiply_add_fusion.1.state_ref, bf16[512,128]{1,0:T(8,128)(2,1)S(1)} %bitcast.31), custom_call_target="tpu_custom_call" | custom-call | flops 1073741824 | bytes 10485760 | tf_op jit(solution)/shard_map/project/pallas_call | solution.py:387
  162.4 1.9 copy-done.1
  164.3 130.6 %triangle_in.1 = bf16[128,64,128]{2,1,0:T(8,128)(2,1)S(1)} custom-call(bf16[8,16,2,64,128]{4,3,2,1,0:T(8,128)(2,1)} %bitcast.34), custom_call_target="tpu_custom_call" | custom-call | flops 2147483648 | bytes 12582912 | tf_op jit(solution)/shard_map/triangle_in/pallas_call | solution.py:280
  294.9 0.6 convert_reduce_fusion
  295.5 0.7 fusion.4
  296.2 0.7 fusion.8
  296.9 3.0 multiply_add_fusion.state_ref
  300.0 11.2 %transition.1 = bf16[128,64,128]{2,1,0:T(8,128)(2,1)} custom-call(f32[64,128,128]{2,1,0:T(8,128)S(1)} %multiply_add_fusion.state_ref, bf16[128,1024]{1,0:T(8,128)(2,1)S(1)} %copy-done.2, bf16[512,128]{1,0:T(8,128)(2,1)S(1)} %copy-done.3), custom_call_target="tpu_custom_call" | custom-call | flops 3221225472 | bytes 6291456 | tf_op jit(solution)/shard_map/transition/pallas_call | solution.py:432
  (17 shorter events, 0.1 us)
Async XLA Ops:
  1.8 1.3 copy-start.6
  1.8 1.3 copy-start.7
  1.8 1.3 copy-start.8
  1.8 1.3 copy-start.9
  16.4 1.9 copy-start
  142.1 1.3 copy-start.4
  143.4 0.8 copy-start.5
  162.4 1.9 copy-start.1
  296.9 3.0 copy-start.2
  296.9 3.0 copy-start.3

commit v2 on v1

--- a/solution.py
+++ b/solution.py
@@ -91,34 +91,34 @@
             ret_local.at[g],
         )
 
-    def along(g, kind, source, target, to):
+    def along(c, kind, source, target, to):
         return pltpu.make_async_remote_copy(
             src_ref=source,
             dst_ref=target,
-            send_sem=z_send.at[kind, g],
-            recv_sem=z_recv.at[kind, g],
+            send_sem=z_send.at[kind, c],
+            recv_sem=z_recv.at[kind, c],
             device_id=(to, col, rep),
             device_id_type=MESH,
         )
 
-    def to_middle(g):
-        if outgoing:
-            return along(g, 0, own.at[group(g), 1], far.at[group(g), 1], mate)
-        return along(g, 0, own.at[group(g)], far.at[group(g)], mate)
-
-    def to_middle_left(g):
-        return along(g, 4, own.at[group(g), 0], far.at[group(g), 0], mate)
-
-    def across_first(g):
-        if outgoing:
-            return along(g, 1, own.at[group(g), 1], inb.at[0, group(g)], across)
-        return along(g, 1, outb.at[group(g)], inb.at[group(g)], across)
-
-    def across_second(g):
-        return along(g, 2, far.at[group(g), 1], inb.at[1, group(g)], across)
-
-    def to_end(g):
-        return along(g, 3, hid.at[far_index, group(g)], got.at[group(g)], mate)
+    def to_middle(c):
+        if outgoing:
+            return along(c, 0, own.at[c, 1], far.at[c, 1], mate)
+        return along(c, 0, own.at[c], far.at[c], mate)
+
+    def to_middle_left(c):
+        return along(c, 4, own.at[c, 0], far.at[c, 0], mate)
+
+    def across_first(c):
+        if outgoing:
+            return along(c, 1, own.at[c, 1], inb.at[0, c], across)
+        return along(c, 1, outb.at[c], inb.at[c], across)
+
+    def across_second(c):
+        return along(c, 2, far.at[c, 1], inb.at[1, c], across)
+
+    def to_end(c):
+        return along(c, 3, hid.at[far_index, c], got.at[c], mate)
 
     def start_spread(g):
         spread_local(g).start()
@@ -187,6 +187,41 @@
     def each(g, func):
         lax.fori_loop(0, per, lambda n, _: (func(g * per + n), _)[1], 0)
 
+    def offer(c):
+        across_first(c).start()
+
+    def pass_on(c):
+        to_middle(c).wait_recv()
+        if outgoing:
+            across_second(c).start()
+        else:
+            forward(c)
+            across_first(c).start()
+
+    def complete(c):
+        across_first(c).wait_recv()
+        if outgoing:
+            to_middle_left(c).wait_recv()
+            across_second(c).wait_recv()
+        multiply(c)
+        to_end(c).start()
+
+    def hand_in(c):
+        to_middle(c).start()
+        if outgoing:
+            to_middle_left(c).start()
+
+    def middle_sent(c):
+        across_first(c).wait_send()
+        if outgoing:
+            across_second(c).wait_send()
+        to_end(c).wait_send()
+
+    def end_sent(c):
+        to_middle(c).wait_send()
+        if outgoing:
+            to_middle_left(c).wait_send()
+
     @pl.when(is_mid)
     def _():
         back = hid.at[own_index]
@@ -196,7 +231,7 @@
             def _():
                 wait_spread(m)
                 if outgoing:
-                    across_first(m).start()
+                    each(m, offer)
 
             @pl.when(m + 1 < groups)
             def _():
@@ -204,24 +239,12 @@
 
             @pl.when((m >= 1) & (m <= groups))
             def _():
-                g = m - 1
-                to_middle(g).wait_recv()
-                if outgoing:
-                    across_second(g).start()
-                else:
-                    each(g, forward)
-                    across_first(g).start()
+                each(m - 1, pass_on)
 
             @pl.when(m >= 2)
             def _():
-                g = m - 2
-                across_first(g).wait_recv()
-                if outgoing:
-                    to_middle_left(g).wait_recv()
-                    across_second(g).wait_recv()
-                each(g, multiply)
-                to_end(g).start()
-                start_back(g, back)
+                each(m - 2, complete)
+                start_back(m - 2, back)
 
             return carry
 
@@ -229,10 +252,7 @@
 
         def drain(g, carry):
             finish_back(g, back)
-            across_first(g).wait_send()
-            if outgoing:
-                across_second(g).wait_send()
-            to_end(g).wait_send()
+            each(g, middle_sent)
             return carry
 
         lax.fori_loop(0, groups, drain, 0)
@@ -243,9 +263,7 @@
             @pl.when(m < groups)
             def _():
                 wait_spread(m)
-                to_middle(m).start()
-                if outgoing:
-                    to_middle_left(m).start()
+                each(m, hand_in)
 
             @pl.when(m + 1 < groups)
             def _():
@@ -253,7 +271,7 @@
 
             @pl.when(m >= LAG)
             def _():
-                to_end(m - LAG).wait_recv()
+                each(m - LAG, lambda c: to_end(c).wait_recv())
                 start_back(m - LAG, got)
 
             return carry
@@ -262,9 +280,7 @@
 
         def drain(g, carry):
             finish_back(g, got)
-            to_middle(g).wait_send()
-            if outgoing:
-                to_middle_left(g).wait_send()
+            each(g, end_sent)
             return carry
 
         lax.fori_loop(0, groups, drain, 0)
@@ -297,8 +313,8 @@
             dma((groups,)),
             dma((groups, members)),
             dma((groups, members)),
-            dma((5, groups)),
-            dma((5, groups)),
+            dma((5, channels)),
+            dma((5, channels)),
         ],
         compiler_params=pltpu.CompilerParams(
             collective_id=1 if outgoing else 2,

time: 311 us -> 306 us (0.984)
  Pallas kernels: 288 us -> 283 us
    pallas_call x2, Pallas kernels: 254 us -> 249 us  [triangle_line(): pl.pallas_call(functools.partial(triangle_kernel, outgoing, cols, reps, g...]
where the time goes in v2:
time: 306 us
  Pallas kernels  283 us (92%)
  matrix products  9.43 us (3%)
  local copies, waits for them, and re-layouts  5.75 us (2%)
  blocking collectives  4.11 us (1%)
  other arithmetic  3.84 us (1%)
    pallas_call x2, Pallas kernels, triangle_line(): pl.pallas_call(functools.partial(triangle_kernel, outgoing, cols, reps, g...  249 us
    pallas_call x2, Pallas kernels, project(): pl.pallas_call(project_kernel, grid=(width // block,), out_shape=(jax.Sha...  22.3 us
    pallas_call x1, Pallas kernels, transition(): pl.pallas_call(transition_kernel, grid=(width // block,), out_shape=jax.S...  11.2 us
    dot_general x2, matrix products, finish(): jnp.einsum('cji,cd->jid', scaled, w_out, preferred_element_type=jnp.float32)  8.06 us

profile of v2, /device:TPU:0, one launch (start us, length us, event | category | flops | bytes accessed | tf_op | source)
XLA Modules:
  0.0 306.2 jit_solution(13893080675712659281)
XLA Ops:
  0.0 1.8 constant_dynamic-slice_fusion
  1.8 0.0 copy-start.6
  1.8 0.0 copy-start.7
  1.8 1.2 convert_bitcast_fusion.state_ref
  3.1 2.1 all_gather.6
  5.2 11.1 %project.2 = (bf16[64,128,128]{2,1,0:T(8,128)(2,1)S(1)}, bf16[128,2,64,128]{3,2,1,0:T(8,128)(2,1)S(1)}) custom-call(f32[64,128,128]{2,1,0:T(8,128)S(1)} %convert_bitcast_fusion.state_ref, bf16[512,128]{1,0:T(8,128)(2,1)S(1)} %bitcast.32), custom_call_target="tpu_custom_call" | custom-call | flops 1073741824 | bytes 10485760 | tf_op jit(solution)/shard_map/project/pallas_call | solution.py:403
  16.4 1.9 copy-done
  18.3 124.0 %triangle_out.1 = bf16[128,64,128]{2,1,0:T(8,128)(2,1)S(1)} custom-call(bf16[8,16,2,64,128]{4,3,2,1,0:T(8,128)(2,1)} %bitcast.33), custom_call_target="tpu_custom_call" | custom-call | flops 2147483648 | bytes 12582912 | tf_op jit(solution)/shard_map/triangle_out/pallas_call | solution.py:296
  142.3 0.0 copy-start.4
  142.3 0.6 convert_reduce_fusion.1
  142.9 0.7 fusion.1
  143.6 0.0 copy-start.5
  143.6 0.7 fusion.10
  144.3 0.1 copy-done.5
  144.4 2.0 all_gather.7
  146.4 5.1 %multiply_add_fusion.1.state_ref = f32[64,128,128]{2,1,0:T(8,128)S(1)} fusion(f32[64,128,128]{2,1,0:T(8,128)S(1)} %fusion.10, bf16[128,64,128]{2,1,0:T(8,128)(2,1)S(1)} %fusion.1, bf16[128,64,128]{2,1,0:T(8,128)(2,1)S(1)} %constant_dynamic-slice_fusion, bf16[2,128,128]{2,1,0:T(8,128)(2,1)S(1)} %all_gather.7), kind=kOutput, calls=%fused_computation.14 | convolution fusion | flops 274726912 | bytes 12615680 | tf_op jit(solution)/shard_map/cji,cd->jid/dot_general | solution.py:369
  151.5 11.1 %project.3 = (bf16[64,128,128]{2,1,0:T(8,128)(2,1)S(1)}, bf16[128,2,64,128]{3,2,1,0:T(8,128)(2,1)S(1)}) custom-call(f32[64,128,128]{2,1,0:T(8,128)S(1)} %multiply_add_fusion.1.state_ref, bf16[512,128]{1,0:T(8,128)(2,1)S(1)} %bitcast.31), custom_call_target="tpu_custom_call" | custom-call | flops 1073741824 | bytes 10485760 | tf_op jit(solution)/shard_map/project/pallas_call | solution.py:403
  162.6 1.9 copy-done.1
  164.5 125.3 %triangle_in.1 = bf16[128,64,128]{2,1,0:T(8,128)(2,1)S(1)} custom-call(bf16[8,16,2,64,128]{4,3,2,1,0:T(8,128)(2,1)} %bitcast.34), custom_call_target="tpu_custom_call" | custom-call | flops 2147483648 | bytes 12582912 | tf_op jit(solution)/shard_map/triangle_in/pallas_call | solution.py:296
  289.8 0.6 convert_reduce_fusion
  290.5 0.7 fusion.4
  291.2 0.7 fusion.8
  291.9 3.0 multiply_add_fusion.state_ref
  294.9 11.2 %transition.1 = bf16[128,64,128]{2,1,0:T(8,128)(2,1)} custom-call(f32[64,128,128]{2,1,0:T(8,128)S(1)} %multiply_add_fusion.state_ref, bf16[128,1024]{1,0:T(8,128)(2,1)S(1)} %copy-done.2, bf16[512,128]{1,0:T(8,128)(2,1)S(1)} %copy-done.3), custom_call_target="tpu_custom_call" | custom-call | flops 3221225472 | bytes 6291456 | tf_op jit(solution)/shard_map/transition/pallas_call | solution.py:448
  (17 shorter events, 0.1 us)
Async XLA Ops:
  1.8 1.3 copy-start.6
  1.8 1.3 copy-start.7
  1.8 1.3 copy-start.8
  1.8 1.3 copy-start.9
  16.4 1.9 copy-start
  142.3 1.3 copy-start.4
  143.6 0.8 copy-start.5
  162.6 1.9 copy-start.1
  291.9 3.0 copy-start.2
  291.9 3.0 copy-start.3
